TPU v7x, 32 devices: a whole 2x2x4 slice. The times are simulated.
32 devices in a mesh: section: 4 (over y, x), expert: 8 (over z, core).
Axes of the slice: x: 2, y: 2, z: 4, core: 2. Of those that a mesh axis runs over, the one named last changes fastest.
Arguments:
- tokens: bfloat16 [4, 128, 4096], P('section', 'expert'), may hold values from -6 to 6
- norm_gain: float32 [4, 4096], P('section'), may hold values from 0.1 to 1.9
- first_routes: int32 [4, 128, 1], P('section', 'expert'), may hold values from 0 to 3; in each aligned block of 16 rows (0 to 15, 16 to 31, ..., all dimensions but the last counted through in order) at most 5 rows name the same one
- first_gates: float32 [4, 128, 1], P('section', 'expert'), may hold values from 0.25 to 2
- second_routes: int32 [4, 128, 1], P('section', 'expert'), may hold values from 0 to 3; in each aligned block of 16 rows (0 to 15, 16 to 31, ..., all dimensions but the last counted through in order) at most 5 rows name the same one
- second_gates: float32 [4, 128, 1], P('section', 'expert'), may hold values from 0.25 to 2
- gate_proj: bfloat16 [4, 8, 4096, 512], P('section', 'expert'), may hold values from -0.09375 to 0.09375
- up_proj: bfloat16 [4, 8, 4096, 512], P('section', 'expert'), may hold values from -0.09375 to 0.09375
- down_proj: bfloat16 [4, 8, 512, 4096], P('section', 'expert'), may hold values from -0.1875 to 0.1875
Outputs:
- mixed: bfloat16 [4, 128, 4096], P('section', 'expert')
Inputs may be any that keep to these rules, and one draw needn't show every extreme that they name: `first_routes`: within the 16 rows of one device, no expert id appears more than 5 times, and in some devices one id appears exactly 5 times. `second_routes`: within the 16 rows of one device, no expert id appears more than 5 times, and in some devices one id appears exactly 5 times.
All inputs are finite; a program needn't handle non-finite values.
Results may differ from a plain program's by a relative error of at most 0.0078.
Values may be sent and summed in bfloat16 or wider, within the bound.
No kernel may reach another device: no remote copies, remote signals or barrier semaphores. Data moves between devices by JAX's collectives and lax.ppermute only.
A program may use at most 64 MiB of HBM per device.

v0:
```python
import jax
import jax.numpy as jnp
from jax import lax
from jax.sharding import PartitionSpec as P

EXPERTS = 4
CAP = 5


EPS = 1e-06


def passed_along(block, axis, distance):
    devices = range(lax.axis_size(axis))
    route = [((i - distance) % len(devices), i) for i in devices]
    return lax.ppermute(block, axis, route)


def normalize(activations, norm_scale):
    values = activations.astype(jnp.float32)
    inv_scale = lax.rsqrt(jnp.mean(values * values, axis=-1, keepdims=True) + EPS)
    return (values * inv_scale * norm_scale[None, :]).astype(jnp.bfloat16)


def moe_update(activations, norm_scale, routes, gate_weight, w_gate, w_up, w_down):
    axis_width = lax.axis_size("expert")
    group_size = axis_width // EXPERTS
    row_count = activations.shape[0]
    model_width = activations.shape[1]
    normed = normalize(activations, norm_scale)
    chosen = routes[:, 0]
    one_hot = (chosen[:, None] == jnp.arange(EXPERTS, dtype=jnp.int32)[None, :]).astype(jnp.int32)
    earlier = jnp.cumsum(one_hot, axis=0) - one_hot
    slot_place = jnp.sum(earlier * one_hot, axis=1)
    target = chosen * CAP + slot_place
    source_row = (
        jnp.full((EXPERTS * CAP,), row_count, jnp.int32)
        .at[target]
        .set(jnp.arange(row_count, dtype=jnp.int32))
    )
    padded = jnp.concatenate([normed, jnp.zeros((1, model_width), jnp.bfloat16)], axis=0)
    packed = padded[source_row].reshape(EXPERTS, CAP, model_width)
    outgoing = jnp.repeat(packed, group_size, axis=0)
    arrived = lax.all_to_all(outgoing, "expert", split_axis=0, concat_axis=0, tiled=True)
    sources = arrived.shape[0]
    items = arrived.shape[1]
    flat = arrived.reshape(sources * items, model_width)
    gate_val = jnp.dot(flat, w_gate, preferred_element_type=jnp.float32)
    up_val = jnp.dot(flat, w_up, preferred_element_type=jnp.float32)
    hidden = (jax.nn.silu(gate_val) * up_val).astype(jnp.bfloat16)
    partial_value = jnp.dot(hidden, w_down, preferred_element_type=jnp.float32).astype(jnp.bfloat16)
    partial_value = partial_value.reshape(sources, items, model_width)
    returned = lax.all_to_all(partial_value, "expert", split_axis=0, concat_axis=0, tiled=True)
    combined = jnp.sum(
        returned.astype(jnp.float32).reshape(EXPERTS, group_size, items, model_width), axis=1
    )
    gathered = combined.reshape(EXPERTS * CAP, model_width)[target]
    return (gate_weight * gathered).astype(jnp.bfloat16)


def add_update(activations, update):
    update = lax.optimization_barrier(update)
    return (activations.astype(jnp.float32) + update.astype(jnp.float32)).astype(jnp.bfloat16)


def on_device(
    tokens,
    norm_gain,
    first_routes,
    first_gates,
    second_routes,
    second_gates,
    gate_proj,
    up_proj,
    down_proj,
):
    inputs_now = tokens[0]
    norm_scale = norm_gain[0]
    w_gate = gate_proj[0, 0]
    w_up = up_proj[0, 0]
    w_down = down_proj[0, 0]
    first_update = moe_update(
        inputs_now, norm_scale, first_routes[0], first_gates[0], w_gate, w_up, w_down
    )
    first_pass = add_update(inputs_now, first_update)
    carried = passed_along(first_pass, "section", 1)
    second_update = moe_update(
        carried, norm_scale, second_routes[0], second_gates[0], w_gate, w_up, w_down
    )
    return add_update(carried, second_update)[None]


def solution(mesh):
    return jax.shard_map(
        on_device,
        mesh=mesh,
        in_specs=(
            P("section", "expert", None),
            P("section", None),
            P("section", "expert", None),
            P("section", "expert", None),
            P("section", "expert", None),
            P("section", "expert", None),
            P("section", "expert", None, None),
            P("section", "expert", None, None),
            P("section", "expert", None, None),
        ),
        out_specs=P("section", "expert", None),
        check_vma=False,
    )
```

profile of v0, /device:TPU:0, one launch (start us, length us, event | category | flops | bytes accessed | tf_op | source)
XLA Modules:
  0.0 111.1 jit_solution(1982754772902081601)
XLA Ops:
  0.0 0.7 fusion.48
  0.8 0.8 select_reduce_fusion.1
  1.6 0.7 fusion.49
  2.3 0.6 scatter_custom_fusion
  2.9 1.1 fusion.30
  4.0 1.0 fusion.32
  5.0 0.6 gather_fusion
  5.8 21.5 %all_to_all.20 = bf16[8,5,4096]{2,1,0:T(8,128)(2,1)S(1)} all-to-all(bf16[8,5,4096]{2,1,0:T(8,128)(2,1)S(1)} %bitcast.67), channel_id=1, replica_groups=mesh['section'=4,'expert'=8] {'expert'}, dimensions={0} | all-to-all | bytes 655360 | tf_op jit(solution)/shard_map/all_to_all | solution.py:44
  27.3 0.1 reshape.122
  27.4 3.0 %fusion.8 = f32[40,512]{1,0:T(8,128)S(1)} fusion(bf16[40,4096]{1,0:T(8,128)(2,1)S(1)} %reshape.122, bf16[1,1,4096,512]{3,2,1,0:T(8,128)(2,1)} %param.15), kind=kOutput, calls=%fused_computation.16 | convolution fusion | flops 167772160 | bytes 4603904 | tf_op jit(solution)/shard_map/dot_general | solution.py:48
  30.4 5.1 %convolution_convert_fusion.1 = bf16[40,4096]{1,0:T(8,128)(2,1)S(1)} fusion(bf16[1,1,512,4096]{3,2,1,0:T(8,128)(2,1)} %param.17, bf16[40,4096]{1,0:T(8,128)(2,1)S(1)} %reshape.122, bf16[1,1,4096,512]{3,2,1,0:T(8,128)(2,1)} %param.16, f32[40,512]{1,0:T(8,128)S(1)} %fusion.8), kind=kOutput, calls=%fused_computation.7 | convolution fusion | flops 335831040 | bytes 9125888 | tf_op jit(solution)/shard_map/dot_general | solution.py:51
  35.6 0.9 reshape.123
  36.5 3.5 %all-to-all-start.1 = ((bf16[8,5,4096]{2,1,0:T(8,128)(2,1)}), bf16[8,5,4096]{2,1,0:T(8,128)(2,1)S(1)}, u32[]{:S(2)}, u32[]{:S(2)}) async-start(bf16[8,5,4096]{2,1,0:T(8,128)(2,1)} %reshape.123), calls=%async_computation.1 | async-start | bytes 1048576 | tf_op jit(solution)/shard_map/all_to_all | solution.py:53
  40.1 0.2 select_reduce_fusion
  40.3 0.6 scatter_custom_fusion.1
  41.0 14.3 %all-to-all-done.1 = bf16[8,5,4096]{2,1,0:T(8,128)(2,1)S(1)} async-done(((bf16[8,5,4096]{2,1,0:T(8,128)(2,1)}), bf16[8,5,4096]{2,1,0:T(8,128)(2,1)S(1)}, u32[]{:S(2)}, u32[]{:S(2)}) %all-to-all-start.1) | async-done | bytes 327712 | tf_op jit(solution)/shard_map/all_to_all | solution.py:53
  55.3 0.1 convert_reduce_fusion.1
  55.5 0.6 gather_fusion.1
  56.3 1.5 %collective-permute-start = (bf16[16,4096]{1,0:T(8,128)(2,1)S(1)}, bf16[16,4096]{1,0:T(8,128)(2,1)S(1)}, u32[]{:S(2)}, u32[]{:S(2)}) collective-permute-start(bf16[16,4096]{1,0:T(8,128)(2,1)S(1)} %fusion.33), channel_id=1, source_target_pairs={{24,0},{0,8},{8,16},{16,24},{25,1},{1,9},{9,17},{17,25},{26,2},{2,... | collective-permute-start | bytes 393224 | tf_op jit(solution)/shard_map/ppermute | solution.py:16
  57.8 4.4 %collective-permute-done = bf16[16,4096]{1,0:T(8,128)(2,1)S(1)} collective-permute-done((bf16[16,4096]{1,0:T(8,128)(2,1)S(1)}, bf16[16,4096]{1,0:T(8,128)(2,1)S(1)}, u32[]{:S(2)}, u32[]{:S(2)}) %collective-permute-start) | collective-permute-done | bytes 131104 | tf_op jit(solution)/shard_map/ppermute | solution.py:16
  62.3 0.1 fusion.26
  62.6 0.6 gather_fusion.2
  63.3 18.1 %all_to_all.21 = bf16[8,5,4096]{2,1,0:T(8,128)(2,1)S(1)} all-to-all(bf16[8,5,4096]{2,1,0:T(8,128)(2,1)S(1)} %bitcast.68), channel_id=1, replica_groups=mesh['section'=4,'expert'=8] {'expert'}, dimensions={0} | all-to-all | bytes 655360 | tf_op jit(solution)/shard_map/all_to_all | solution.py:44
  81.4 0.1 reshape.129
  81.6 3.0 %fusion.6 = f32[40,512]{1,0:T(8,128)S(1)} fusion(bf16[40,4096]{1,0:T(8,128)(2,1)S(1)} %reshape.129, bf16[1,1,4096,512]{3,2,1,0:T(8,128)(2,1)} %param.15), kind=kOutput, calls=%fused_computation.14 | convolution fusion | flops 167772160 | bytes 4603904 | tf_op jit(solution)/shard_map/dot_general | solution.py:48
  84.6 5.1 %convolution_convert_fusion = bf16[40,4096]{1,0:T(8,128)(2,1)S(1)} fusion(bf16[1,1,512,4096]{3,2,1,0:T(8,128)(2,1)} %param.17, bf16[40,4096]{1,0:T(8,128)(2,1)S(1)} %reshape.129, bf16[1,1,4096,512]{3,2,1,0:T(8,128)(2,1)} %param.16, f32[40,512]{1,0:T(8,128)S(1)} %fusion.6), kind=kOutput, calls=%fused_computation.6 | convolution fusion | flops 335831040 | bytes 9125888 | tf_op jit(solution)/shard_map/dot_general | solution.py:51
  89.7 0.9 reshape.130
  90.7 3.5 %all-to-all-start.3 = ((bf16[8,5,4096]{2,1,0:T(8,128)(2,1)}), bf16[8,5,4096]{2,1,0:T(8,128)(2,1)S(1)}, u32[]{:S(2)}, u32[]{:S(2)}) async-start(bf16[8,5,4096]{2,1,0:T(8,128)(2,1)} %reshape.130), calls=%async_computation.3 | async-start | bytes 1048576 | tf_op jit(solution)/shard_map/all_to_all | solution.py:53
  94.2 15.3 %all-to-all-done.3 = bf16[8,5,4096]{2,1,0:T(8,128)(2,1)S(1)} async-done(((bf16[8,5,4096]{2,1,0:T(8,128)(2,1)}), bf16[8,5,4096]{2,1,0:T(8,128)(2,1)S(1)}, u32[]{:S(2)}, u32[]{:S(2)}) %all-to-all-start.3) | async-done | bytes 327712 | tf_op jit(solution)/shard_map/all_to_all | solution.py:53
  109.4 0.1 convert_reduce_fusion
  109.6 0.6 gather_fusion.3
  110.4 0.7 fusion.34
  (36 shorter events, 0.9 us)
Async XLA Ops:
  30.4 9.6 %copy-start.2 = (s32[1,16,1]{1,2,0:T(1,128)S(1)}, s32[1,16,1]{1,2,0:T(1,128)}, u32[]{:S(2)}) copy-start(s32[1,16,1]{1,2,0:T(1,128)} %param.13) | copy-start | bytes 196
  35.6 20.6 %copy-start.3 = (f32[1,16,1]{1,2,0:T(1,128)S(1)}, f32[1,16,1]{1,2,0:T(1,128)}, u32[]{:S(2)}) copy-start(f32[1,16,1]{1,2,0:T(1,128)} %param.12) | copy-start | bytes 196
  35.6 20.7 %copy-start = (bf16[1,16,4096]{2,1,0:T(8,128)(2,1)S(1)}, bf16[1,16,4096]{2,1,0:T(8,128)(2,1)}, u32[]{:S(2)}) copy-start(bf16[1,16,4096]{2,1,0:T(8,128)(2,1)} %param.9) | copy-start | bytes 393220
  35.6 26.8 %copy-start.1 = (f32[1,4096]{1,0:T(1,128)S(1)}, f32[1,4096]{1,0:T(1,128)}, u32[]{:S(2)}) copy-start(f32[1,4096]{1,0:T(1,128)} %param.10) | copy-start | bytes 49156
  36.5 18.8 %all-to-all-start.1 = ((bf16[8,5,4096]{2,1,0:T(8,128)(2,1)}), bf16[8,5,4096]{2,1,0:T(8,128)(2,1)S(1)}, u32[]{:S(2)}, u32[]{:S(2)}) async-start(bf16[8,5,4096]{2,1,0:T(8,128)(2,1)} %reshape.123), calls=%async_computation.1 | async-start | bytes 1048576 | tf_op jit(solution)/shard_map/all_to_all | solution.py:53
  56.3 6.0 %collective-permute-start = (bf16[16,4096]{1,0:T(8,128)(2,1)S(1)}, bf16[16,4096]{1,0:T(8,128)(2,1)S(1)}, u32[]{:S(2)}, u32[]{:S(2)}) collective-permute-start(bf16[16,4096]{1,0:T(8,128)(2,1)S(1)} %fusion.33), channel_id=1, source_target_pairs={{24,0},{0,8},{8,16},{16,24},{25,1},{1,9},{9,17},{17,25},{26,2},{2,... | collective-permute-start | bytes 393224 | tf_op jit(solution)/shard_map/ppermute | solution.py:16
  89.7 20.5 %copy-start.4 = (f32[1,16,1]{1,2,0:T(1,128)S(1)}, f32[1,16,1]{1,2,0:T(1,128)}, u32[]{:S(2)}) copy-start(f32[1,16,1]{1,2,0:T(1,128)} %param.14) | copy-start | bytes 196
  90.7 18.8 %all-to-all-start.3 = ((bf16[8,5,4096]{2,1,0:T(8,128)(2,1)}), bf16[8,5,4096]{2,1,0:T(8,128)(2,1)S(1)}, u32[]{:S(2)}, u32[]{:S(2)}) async-start(bf16[8,5,4096]{2,1,0:T(8,128)(2,1)} %reshape.130), calls=%async_computation.3 | async-start | bytes 1048576 | tf_op jit(solution)/shard_map/all_to_all | solution.py:53
where the time goes:
time: 112 us; the launch traced here: 111 us
  blocking collectives  39.6 us (35%)
  waiting for transfers between devices  34 us (30%)
  matrix products  16.2 us (14%)
  starting transfers between devices  8.53 us (8%)
  local copies, waits for them, and re-layouts  6.36 us (6%)
  other arithmetic  6.03 us (5%)
    all_to_all x2, blocking collectives, moe_update(): lax.all_to_all(outgoing, 'expert', split_axis=0, concat_axis=0, tiled=True)  39.6 us
    all_to_all x2, waiting for transfers between devices, moe_update(): lax.all_to_all(partial_value, 'expert', split_axis=0, concat_axis=0, tile...  29.6 us
    dot_general x2, matrix products, moe_update(): jnp.dot(hidden, w_down, preferred_element_type=jnp.float32)  10.2 us
    all_to_all x2, starting transfers between devices, moe_update(): lax.all_to_all(partial_value, 'expert', split_axis=0, concat_axis=0, tile...  6.98 us
    dot_general x2, matrix products, moe_update(): gate_val = jnp.dot(flat, w_gate, preferred_element_type=jnp.float32)  6 us
    ppermute x1, waiting for transfers between devices, passed_along(): return lax.ppermute(block, axis, route)  4.43 us
  transfers between devices with their start and end apart: 3, of which 3 were waited for; matrix products, arithmetic and copies ran while one was open for 1% of the time, Pallas kernels for 0%

commit v1 on v0

v1 whole, which is shorter than its diff:
```python
import jax
import jax.numpy as jnp
from jax import lax
from jax.sharding import PartitionSpec as P

EXPERTS = 4
EPS = 1e-06


def normalize(activations, norm_scale):
    values = activations.astype(jnp.float32)
    inv_scale = lax.rsqrt(jnp.mean(values * values, axis=-1, keepdims=True) + EPS)
    return (values * inv_scale * norm_scale[None, :]).astype(jnp.bfloat16)


def layer(rows, norm_scale, routes, gates, w_gate, w_up, w_down):
    width = rows.shape[1]
    group = lax.axis_size("expert") // EXPERTS
    mine = lax.axis_index("expert") // group
    normed = normalize(rows, norm_scale)
    ids = jnp.broadcast_to(routes.astype(jnp.bfloat16), (rows.shape[0], 128))
    everyone = lax.all_gather(
        jnp.concatenate([normed, ids], axis=1), "expert", axis=0, tiled=True
    )
    here = everyone[:, width : width + 1] == mine.astype(jnp.bfloat16)
    values = everyone[:, :width]
    gate_val = jnp.dot(values, w_gate, preferred_element_type=jnp.float32)
    up_val = jnp.dot(values, w_up, preferred_element_type=jnp.float32)
    hidden = jnp.where(here, jax.nn.silu(gate_val) * up_val, 0.0).astype(jnp.bfloat16)
    partial_value = jnp.dot(hidden, w_down, preferred_element_type=jnp.float32)
    summed = lax.psum_scatter(
        partial_value.astype(jnp.bfloat16), "expert", scatter_dimension=0, tiled=True
    )
    update = (gates * summed.astype(jnp.float32)).astype(jnp.bfloat16)
    return (rows.astype(jnp.float32) + update.astype(jnp.float32)).astype(jnp.bfloat16)


def on_device(tokens, gain, routes_1, gates_1, routes_2, gates_2, gate_proj, up_proj, down_proj):
    sections = lax.axis_size("section")
    weights = (gate_proj[0, 0], up_proj[0, 0], down_proj[0, 0])
    first = layer(tokens[0], gain[0], routes_1[0], gates_1[0], *weights)
    carried = lax.ppermute(first, "section", [(i, (i + 1) % sections) for i in range(sections)])
    return layer(carried, gain[0], routes_2[0], gates_2[0], *weights)[None]


def solution(mesh):
    rows = P("section", "expert", None)
    slabs = P("section", "expert", None, None)
    return jax.shard_map(
        on_device,
        mesh=mesh,
        in_specs=(rows, P("section", None), rows, rows, rows, rows, slabs, slabs, slabs),
        out_specs=rows,
        check_vma=False,
    )
```

time: 112 us -> 156 us (1.39)
  waiting for transfers between devices: 34 us -> 113 us
  blocking collectives: 39.6 us -> 0 us
  between operations: 0.31 us -> 13.3 us
  starting transfers between devices: 8.53 us -> 1.97 us
  local copies, waits for them, and re-layouts: 6.36 us -> 0.18 us
  other arithmetic: 6.03 us -> 8.89 us
  matrix products: 16.2 us -> 18.2 us
    reduce_scatter x0 -> x2, waiting for transfers between devices: none -> 63.9 us  [layer(): lax.psum_scatter(partial_value.astype(jnp.bfloat16), 'expert', scatter_di...]
    all_gather x0 -> x2, waiting for transfers between devices: none -> 45.3 us  [layer(): lax.all_gather(jnp.concatenate([normed, ids], axis=1), 'expert', axis=0,...]
    all_to_all x2 -> x0, blocking collectives: 39.6 us -> none  [moe_update(): lax.all_to_all(outgoing, 'expert', split_axis=0, concat_axis=0, tiled=True)]
    all_to_all x2 -> x0, waiting for transfers between devices: 29.6 us -> none  [moe_update(): lax.all_to_all(partial_value, 'expert', split_axis=0, concat_axis=0, tile...]
    all_to_all x2 -> x0, starting transfers between devices: 6.98 us -> none  [moe_update(): lax.all_to_all(partial_value, 'expert', split_axis=0, concat_axis=0, tile...]
    gather x4 -> x0, local copies, waits for them, and re-layouts: 2.58 us -> none  [the longest x2 1.29 us: moe_update(): packed = padded[source_row].reshape(EXPERTS, CAP, model_width)]
    reshape x8 -> x0, local copies, waits for them, and re-layouts: 2.41 us -> none  [the longest x2 1.85 us: moe_update(): partial_value = partial_value.reshape(sources, items, model_width)]
    dot_general x4, matrix products: 16.2 us -> 18.2 us  [the longest x2 11.7 us: layer(): partial_value = jnp.dot(hidden, w_down, preferred_element_type=jnp.float32)]
  transfers between devices with their start and end apart: 3 -> 5, of which waited for: 3 -> 5; matrix products, arithmetic and copies ran while one was open for 1% -> 0% of each run, Pallas kernels for 0% -> 0%
where the time goes in v1:
time: 156 us
  waiting for transfers between devices  113 us (72%)
  matrix products  18.2 us (12%)
  between operations  13.3 us (9%)
  other arithmetic  8.89 us (6%)
  starting transfers between devices  1.97 us (1%)
    reduce_scatter x2, waiting for transfers between devices, layer(): lax.psum_scatter(partial_value.astype(jnp.bfloat16), 'expert', scatter_di...  63.9 us
    all_gather x2, waiting for transfers between devices, layer(): lax.all_gather(jnp.concatenate([normed, ids], axis=1), 'expert', axis=0,...  45.3 us
    dot_general x2, matrix products, layer(): partial_value = jnp.dot(hidden, w_down, preferred_element_type=jnp.float32)  11.7 us
    dot_general x2, matrix products, layer(): gate_val = jnp.dot(values, w_gate, preferred_element_type=jnp.float32)  6.47 us
    ppermute x1, waiting for transfers between devices, on_device(): lax.ppermute(first, 'section', [(i, (i + 1) % sections) for i in range(se...  4.07 us
  transfers between devices with their start and end apart: 5, of which 5 were waited for; matrix products, arithmetic and copies ran while one was open for 0% of the time, Pallas kernels for 0%

profile of v1, /device:TPU:0, one launch (start us, length us, event | category | flops | bytes accessed | tf_op | source)
XLA Modules:
  0.0 155.8 jit_solution(1248726703301738748)
XLA Ops:
  6.5 0.7 convert_bitcast_fusion.1
  7.2 1.0 fusion.44
  8.3 1.0 fusion.46
  9.3 0.1 broadcast_in_dim.37
  9.3 0.7 pad_maximum_fusion
  10.0 0.0 all-gather.3.cloned.1.call-update
  10.0 0.0 reduce-scatter.3.cloned.1.call-start
  10.1 25.1 %all-gather.3.cloned.1.call-done = bf16[128,4224]{1,0:T(8,128)(2,1)} async-done(((bf16[16,4224]{1,0:T(8,128)(2,1)}), bf16[128,4224]{1,0:T(8,128)(2,1)}) %all-gather.3.cloned.1.call-update) | async-done | bytes 1081360 | tf_op jit(solution)/shard_map/all_gather | solution.py:22
  35.2 1.0 compare_reduce_fusion.1
  36.1 3.2 %fusion.8 = f32[128,512]{1,0:T(8,128)S(1)} fusion(bf16[1,1,4096,512]{3,2,1,0:T(8,128)(2,1)} %param.15, bf16[128,4224]{1,0:T(8,128)(2,1)} %all-gather.3.cloned.1.call-done), kind=kOutput, calls=%fused_computation.10 | convolution fusion | flops 536870912 | bytes 5505024 | tf_op jit(solution)/shard_map/dot_general | solution.py:27
  39.4 0.0 copy-start.2
  39.4 0.0 copy-start.3
  39.4 5.9 %convolution_convert_fusion.1 = bf16[128,4096]{1,0:T(8,128)(2,1)} fusion(bf16[1,1,512,4096]{3,2,1,0:T(8,128)(2,1)} %param.17, bf16[1,1,4096,512]{3,2,1,0:T(8,128)(2,1)} %param.16, bf16[128,4224]{1,0:T(8,128)(2,1)S(1)} %copy-done, f32[128,512]{1,0:T(8,128)S(1)} %fusion.8, pred[128]{0:T(512)(128)(4,1)S(1)} %compare_reduce_fusion.1), kind=kOutput, calls=%fused_computation.1 | convolution fusion | flops 1074724864 | bytes 10748416 | tf_op jit(solution)/shard_map/dot_general | solution.py:30
  45.3 0.0 reduce-scatter.3.cloned.1.call-update
  45.4 0.0 all-gather.5.cloned.1.call-start
  45.4 31.9 %reduce-scatter.3.cloned.1.call-done = bf16[16,4096]{1,0:T(8,128)(2,1)} async-done(((bf16[128,4096]{1,0:T(8,128)(2,1)}), bf16[16,4096]{1,0:T(8,128)(2,1)}) %reduce-scatter.3.cloned.1.call-update) | async-done | bytes 131088 | tf_op jit(solution)/shard_map/reduce_scatter | solution.py:31
  77.3 1.0 fusion.47
  78.3 1.8 %collective-permute-start = (bf16[16,4096]{1,0:T(8,128)(2,1)S(1)}, bf16[16,4096]{1,0:T(8,128)(2,1)S(1)}, u32[]{:S(2)}, u32[]{:S(2)}) collective-permute-start(bf16[16,4096]{1,0:T(8,128)(2,1)S(1)} %fusion.47), channel_id=1, source_target_pairs={{0,8},{8,16},{16,24},{24,0},{1,9},{9,17},{17,25},{25,1},{2,10},{10... | collective-permute-start | bytes 393224 | tf_op jit(solution)/shard_map/ppermute | solution.py:42
  80.2 4.1 %collective-permute-done = bf16[16,4096]{1,0:T(8,128)(2,1)S(1)} collective-permute-done((bf16[16,4096]{1,0:T(8,128)(2,1)S(1)}, bf16[16,4096]{1,0:T(8,128)(2,1)S(1)}, u32[]{:S(2)}, u32[]{:S(2)}) %collective-permute-start) | collective-permute-done | bytes 131104 | tf_op jit(solution)/shard_map/ppermute | solution.py:42
  84.2 0.1 fusion.40
  84.4 0.1 fusion.42
  84.5 0.1 broadcast_in_dim.41
  84.6 0.7 pad_maximum_fusion.1
  85.2 0.0 all-gather.5.cloned.1.call-update
  85.3 0.0 reduce-scatter.5.cloned.1.call-start
  85.3 20.2 %all-gather.5.cloned.1.call-done = bf16[128,4224]{1,0:T(8,128)(2,1)} async-done(((bf16[16,4224]{1,0:T(8,128)(2,1)}), bf16[128,4224]{1,0:T(8,128)(2,1)}) %all-gather.5.cloned.1.call-update) | async-done | bytes 1081360 | tf_op jit(solution)/shard_map/all_gather | solution.py:22
  105.5 1.0 compare_reduce_fusion
  106.5 3.2 %fusion.6 = f32[128,512]{1,0:T(8,128)S(1)} fusion(bf16[1,1,4096,512]{3,2,1,0:T(8,128)(2,1)} %param.15, bf16[128,4224]{1,0:T(8,128)(2,1)} %all-gather.5.cloned.1.call-done), kind=kOutput, calls=%fused_computation.8 | convolution fusion | flops 536870912 | bytes 5505024 | tf_op jit(solution)/shard_map/dot_general | solution.py:27
  109.8 5.8 %convolution_convert_fusion = bf16[128,4096]{1,0:T(8,128)(2,1)} fusion(bf16[1,1,512,4096]{3,2,1,0:T(8,128)(2,1)} %param.17, bf16[1,1,4096,512]{3,2,1,0:T(8,128)(2,1)} %param.16, bf16[128,4224]{1,0:T(8,128)(2,1)S(1)} %copy-done.1, f32[128,512]{1,0:T(8,128)S(1)} %fusion.6, pred[128]{0:T(512)(128)(4,1)S(1)} %compare_reduce_fusion), kind=kOutput, calls=%fused_computation | convolution fusion | flops 1074724864 | bytes 10748416 | tf_op jit(solution)/shard_map/dot_general | solution.py:30
  115.6 0.0 reduce-scatter.5.cloned.1.call-update
  115.6 32.0 %reduce-scatter.5.cloned.1.call-done = bf16[16,4096]{1,0:T(8,128)(2,1)} async-done(((bf16[128,4096]{1,0:T(8,128)(2,1)}), bf16[16,4096]{1,0:T(8,128)(2,1)}) %reduce-scatter.5.cloned.1.call-update) | async-done | bytes 131088 | tf_op jit(solution)/shard_map/reduce_scatter | solution.py:31
  147.6 1.7 %fusion.58 = bf16[1,16,4096]{2,1,0:T(8,128)(2,1)} fusion(bf16[16,4096]{1,0:T(8,128)(2,1)} %reduce-scatter.5.cloned.1.call-done, bf16[16,4096]{1,0:T(8,128)(2,1)S(1)} %collective-permute-done, f32[16]{0:T(128)S(1)} %bitcast.48), kind=kLoop, calls=%fused_computation.50 | loop fusion | flops 458752 | bytes 393280 | tf_op jit(solution)/shard_map/broadcast_in_dim | solution.py:43
  (16 shorter events, 0.1 us)
Async XLA Ops:
  6.5 28.6 %all-gather.3.cloned.1.call-start = ((), (), s32[]{:S(2)}) async-start(), calls=%async_computation.2 | async-start | bytes 1216512 | tf_op jit(solution)/shard_map/all_gather | solution.py:22
  10.0 67.3 %reduce-scatter.3.cloned.1.call-start = ((), (), s32[]{:S(2)}) async-start(), calls=%async_computation.3 | async-start | bytes 1179648 | tf_op jit(solution)/shard_map/reduce_scatter | solution.py:31
  35.2 4.2 %copy-start = (bf16[128,4224]{1,0:T(8,128)(2,1)S(1)}, bf16[128,4224]{1,0:T(8,128)(2,1)}, u32[]{:S(2)}) copy-start(bf16[128,4224]{1,0:T(8,128)(2,1)} %all-gather.3.cloned.1.call-done) | copy-start | bytes 3244036
  39.4 37.9 %copy-start.2 = (bf16[1,16,4096]{2,1,0:T(8,128)(2,1)S(1)}, bf16[1,16,4096]{2,1,0:T(8,128)(2,1)}, u32[]{:S(2)}) copy-start(bf16[1,16,4096]{2,1,0:T(8,128)(2,1)} %param.9) | copy-start | bytes 393220
  39.4 37.9 %copy-start.4 = (f32[1,16,1]{1,2,0:T(1,128)S(1)}, f32[1,16,1]{1,2,0:T(1,128)}, u32[]{:S(2)}) copy-start(f32[1,16,1]{1,2,0:T(1,128)} %param.12) | copy-start | bytes 196
  39.4 40.7 %copy-start.6 = (s32[1,16,1]{1,2,0:T(1,128)S(1)}, s32[1,16,1]{1,2,0:T(1,128)}, u32[]{:S(2)}) copy-start(s32[1,16,1]{1,2,0:T(1,128)} %param.13) | copy-start | bytes 196
  39.4 45.0 %copy-start.3 = (f32[1,4096]{1,0:T(1,128)S(1)}, f32[1,4096]{1,0:T(1,128)}, u32[]{:S(2)}) copy-start(f32[1,4096]{1,0:T(1,128)} %param.10) | copy-start | bytes 49156
  45.4 60.2 %all-gather.5.cloned.1.call-start = ((), (), s32[]{:S(2)}) async-start(), calls=%async_computation.4 | async-start | bytes 1216512 | tf_op jit(solution)/shard_map/all_gather | solution.py:22
  78.3 5.9 %collective-permute-start = (bf16[16,4096]{1,0:T(8,128)(2,1)S(1)}, bf16[16,4096]{1,0:T(8,128)(2,1)S(1)}, u32[]{:S(2)}, u32[]{:S(2)}) collective-permute-start(bf16[16,4096]{1,0:T(8,128)(2,1)S(1)} %fusion.47), channel_id=1, source_target_pairs={{0,8},{8,16},{16,24},{24,0},{1,9},{9,17},{17,25},{25,1},{2,10},{10... | collective-permute-start | bytes 393224 | tf_op jit(solution)/shard_map/ppermute | solution.py:42
  85.3 62.4 %reduce-scatter.5.cloned.1.call-start = ((), (), s32[]{:S(2)}) async-start(), calls=%async_computation.5 | async-start | bytes 1179648 | tf_op jit(solution)/shard_map/reduce_scatter | solution.py:31
  105.5 4.2 %copy-start.1 = (bf16[128,4224]{1,0:T(8,128)(2,1)S(1)}, bf16[128,4224]{1,0:T(8,128)(2,1)}, u32[]{:S(2)}) copy-start(bf16[128,4224]{1,0:T(8,128)(2,1)} %all-gather.5.cloned.1.call-done) | copy-start | bytes 3244036
  109.8 37.9 %copy-start.5 = (f32[1,16,1]{1,2,0:T(1,128)S(1)}, f32[1,16,1]{1,2,0:T(1,128)}, u32[]{:S(2)}) copy-start(f32[1,16,1]{1,2,0:T(1,128)} %param.14) | copy-start | bytes 196
Sparse Core Ops, SparseCore 0:
  10.1 24.9 all-gather.2
  45.5 31.7 reduce-scatter.2
  85.4 20.1 all-gather.4
  115.7 31.8 reduce-scatter.4

commit v2 on v1

v2 whole, which is shorter than its diff:
```python
import functools

import jax
import jax.numpy as jnp
from jax import lax
from jax.experimental import pallas as pl
from jax.experimental.pallas import tpu as pltpu
from jax.sharding import PartitionSpec as P

EXPERTS = 4
CAP = 5
ROWS = 16
CHUNKS = 3
EPS = 1e-06
F32 = jnp.float32
BF16 = jnp.bfloat16
VMEM = pl.BlockSpec(memory_space=pltpu.VMEM)


def fifth(value):
    return (value * 205) >> 10


def chunk_width(width):
    return -(-width // (CHUNKS * 128)) * 128


def chunk_span(width, chunk):
    start = chunk * chunk_width(width)
    return start, min(width, start + chunk_width(width)) - start


def upright(row):
    rows = row.shape[1]
    same = lax.broadcasted_iota(jnp.int32, (rows, rows), 0) == lax.broadcasted_iota(
        jnp.int32, (rows, rows), 1
    )
    return jnp.sum(jnp.where(same, row, 0.0), axis=1, keepdims=True)


def slots_of(routes):
    rows = routes.shape[0]
    lanes = lax.broadcasted_iota(jnp.int32, (rows, 128), 1).astype(F32)
    one_hot = (routes == lanes).astype(F32)
    earlier = lax.broadcasted_iota(jnp.int32, (rows, rows), 0) > lax.broadcasted_iota(
        jnp.int32, (rows, rows), 1
    )
    before = jnp.dot(earlier.astype(BF16), one_hot.astype(BF16), preferred_element_type=F32)
    return routes * CAP + jnp.sum(before * one_hot, axis=1, keepdims=True)


def block_map(slots, expert, chunk):
    spot = lax.broadcasted_iota(jnp.int32, (slots.shape[0], EXPERTS * ROWS), 1)
    inner = (spot & (ROWS - 1)) - CAP * chunk
    target = ((spot >> 4) ^ expert) * CAP + inner
    target = jnp.where((inner >= 0) & (inner < CAP), target, -1)
    return (slots == target.astype(F32)).astype(BF16)


def normalize(values, gain):
    inv_scale = lax.rsqrt(jnp.mean(values * values, axis=-1, keepdims=True) + EPS)
    return (values * inv_scale * gain).astype(BF16)


def write_blocks(normed, slots, expert, block_refs):
    width = normed.shape[1]
    pieces = []
    for chunk in range(CHUNKS):
        start, span = chunk_span(width, chunk)
        piece = lax.dot_general(
            block_map(slots, expert, chunk),
            normed[:, start : start + span],
            (((0,), (0,)), ((), ())),
            preferred_element_type=F32,
        )
        if span < chunk_width(width):
            piece = jnp.concatenate(
                [piece, jnp.zeros((piece.shape[0], chunk_width(width) - span), F32)], axis=1
            )
        pieces.append(piece)
    packed = sum(pieces[1:], pieces[0]).astype(BF16)
    for k, ref in enumerate(block_refs):
        ref[...] = packed[k * ROWS : (k + 1) * ROWS]


def my_expert(group):
    return lax.axis_index("expert") // group


def pack_kernel(group, x_ref, gain_ref, routes_ref, gates_ref, meta_ref, *block_refs):
    slots = slots_of(upright(routes_ref[...].astype(F32)))
    gates = upright(gates_ref[...])
    lane = lax.broadcasted_iota(jnp.int32, meta_ref.shape, 1)
    meta_ref[...] = jnp.where(lane == 0, slots, jnp.where(lane == 1, gates, 0.0))
    normed = normalize(x_ref[...].astype(F32), gain_ref[...])
    write_blocks(normed, slots, my_expert(group), block_refs)


def residual(x, slots, gates, expert, blocks):
    width = x.shape[1]
    found = []
    for chunk in range(CHUNKS):
        _, span = chunk_span(width, chunk)
        found.append(
            jnp.dot(
                block_map(slots, expert, chunk), blocks[:, :span], preferred_element_type=F32
            )
        )
    update = (gates * jnp.concatenate(found, axis=1)).astype(BF16)
    return x.astype(F32) + update.astype(F32)


def middle_kernel(group, x_ref, meta_ref, b0, b1, b2, b3, gain_ref, routes_ref, first_ref, *block_refs):
    blocks = jnp.concatenate([b0[...], b1[...], b2[...], b3[...]], axis=0)
    expert = my_expert(group)
    first = residual(x_ref[...], meta_ref[:, 0:1], meta_ref[:, 1:2], expert, blocks).astype(BF16)
    first_ref[...] = first
    slots = slots_of(upright(routes_ref[...].astype(F32)))
    normed = normalize(first.astype(F32), gain_ref[...])
    write_blocks(normed, slots, expert, block_refs)


def last_kernel(group, x_ref, b0, b1, b2, b3, routes_ref, gates_ref, out_ref):
    blocks = jnp.concatenate([b0[...], b1[...], b2[...], b3[...]], axis=0)
    slots = slots_of(upright(routes_ref[...].astype(F32)))
    gates = upright(gates_ref[...])
    out_ref[...] = residual(x_ref[...], slots, gates, my_expert(group), blocks).astype(BF16)


def compact_map(shape, compact_dim, chunk):
    compact = lax.broadcasted_iota(jnp.int32, shape, compact_dim)
    spot = lax.broadcasted_iota(jnp.int32, shape, 1 - compact_dim)
    block = fifth(compact)
    wanted = block * ROWS + CAP * chunk + compact - CAP * block
    return (wanted == spot).astype(BF16)


def expert_kernel(count, w_gate, w_up, w_down, *refs):
    ins, outs, (x_ref, part_ref) = refs[:count], refs[count:-2], refs[-2:]
    width, units = w_gate.shape
    rows = x_ref.shape[0]
    blocks = jnp.concatenate([ref[...] for ref in ins], axis=0)
    for chunk in range(CHUNKS):
        start, span = chunk_span(width, chunk)
        x_ref[:, start : start + span] = jnp.dot(
            compact_map((rows, count * ROWS), 0, chunk),
            blocks[:, :span],
            preferred_element_type=F32,
        ).astype(BF16)
    x = x_ref[...]
    gate_val = jnp.dot(x, w_gate[...], preferred_element_type=F32)
    up_val = jnp.dot(x, w_up[...], preferred_element_type=F32)
    hidden = (gate_val / (1.0 + jnp.exp(-gate_val)) * up_val).astype(BF16)
    part_ref[...] = jnp.dot(hidden, w_down[...], preferred_element_type=F32).astype(BF16)
    total = None
    for chunk in range(CHUNKS):
        start, span = chunk_span(width, chunk)
        piece = jnp.dot(
            compact_map((count * ROWS, rows), 1, chunk),
            part_ref[:, start : start + span],
            preferred_element_type=F32,
        )
        if span < chunk_width(width):
            piece = jnp.concatenate(
                [piece, jnp.zeros((piece.shape[0], chunk_width(width) - span), F32)], axis=1
            )
        total = piece if total is None else total + piece
    total = total.astype(BF16)
    for m, ref in enumerate(outs):
        ref[...] = total[m * EXPERTS * ROWS : (m + 1) * EXPERTS * ROWS]


def sum_kernel(*refs):
    ins, outs = refs[:-EXPERTS], refs[-EXPERTS:]
    total = ins[0][...].astype(F32)
    for ref in ins[1:]:
        total = total + ref[...].astype(F32)
    total = total.astype(BF16)
    for k, ref in enumerate(outs):
        ref[...] = total[k * ROWS : (k + 1) * ROWS]


def call(body, outs, ins, megabytes, scratch=(), flops=0):
    moved = sum(a.size * a.dtype.itemsize for a in (*ins, *outs))
    return pl.pallas_call(
        body,
        out_shape=outs,
        in_specs=[VMEM] * len(ins),
        out_specs=[VMEM] * len(outs),
        scratch_shapes=list(scratch),
        compiler_params=pltpu.CompilerParams(vmem_limit_bytes=megabytes << 20),
        cost_estimate=pl.CostEstimate(flops=flops, bytes_accessed=moved, transcendentals=0),
    )(*ins)


def on_device(tokens, gain, routes_1, gates_1, routes_2, gates_2, gate_proj, up_proj, down_proj):
    sections, devices = lax.axis_size("section"), lax.axis_size("expert")
    group = devices // EXPERTS
    rows, width = tokens.shape[1:]
    weights = (gate_proj[0, 0], up_proj[0, 0], down_proj[0, 0])
    wide = chunk_width(width)
    block = jax.ShapeDtypeStruct((ROWS, wide), BF16)
    stack = jax.ShapeDtypeStruct((EXPERTS * ROWS, wide), BF16)
    whole = jax.ShapeDtypeStruct((rows, width), BF16)
    meta = jax.ShapeDtypeStruct((rows, 128), F32)
    routes_1, gates_1, routes_2, gates_2 = (
        a.reshape(1, rows) for a in (routes_1, gates_1, routes_2, gates_2)
    )

    def to_expert(k):
        return [(i, (i // group ^ k) * group + i % group) for i in range(devices)]

    def within(shift):
        return [(i, i // group * group + (i + shift) % group) for i in range(devices)]

    def onward(k):
        return [
            (s * devices + i, (s + 1) % sections * devices + j)
            for s in range(sections)
            for i, j in to_expert(k)
        ]

    def experts(blocks):
        arrived = [None] * EXPERTS
        for k in (3, 2, 1):
            arrived[k] = lax.ppermute(blocks[k], "expert", to_expert(k))
        arrived[0] = blocks[0]
        ins = list(arrived)
        for m in range(1, group):
            ins += [lax.ppermute(a, "expert", within(m)) for a in arrived]
        count = EXPERTS * group
        held = -(-count * CAP // ROWS) * ROWS
        sums = call(
            functools.partial(expert_kernel, count),
            [stack] * group,
            [*weights, *ins],
            24,
            [pltpu.VMEM((held, width), BF16), pltpu.VMEM((held, width), BF16)],
            flops=6 * held * width * weights[0].shape[1],
        )
        terms = [sums[0]] + [lax.ppermute(sums[m], "expert", within(-m)) for m in range(1, group)]
        return call(sum_kernel, [block] * EXPERTS, terms, 8)

    slots, *blocks = call(
        functools.partial(pack_kernel, group),
        [meta] + [block] * EXPERTS,
        [tokens[0], gain, routes_1, gates_1],
        8,
    )
    ahead = [(i, (i + 1) % sections) for i in range(sections)]
    slots = lax.ppermute(slots, "section", ahead)
    before = lax.ppermute(tokens[0], "section", ahead)
    sums = experts(blocks)
    home = [lax.ppermute(sums[k], ("section", "expert"), onward(k)) for k in range(EXPERTS)]
    first, *blocks = call(
        functools.partial(middle_kernel, group),
        [whole] + [block] * EXPERTS,
        [before, slots, *home, gain, routes_2],
        8,
    )
    sums = experts(blocks)
    home = [sums[0]] + [lax.ppermute(sums[k], "expert", to_expert(k)) for k in (1, 2, 3)]
    (mixed,) = call(
        functools.partial(last_kernel, group), [whole], [first, *home, routes_2, gates_2], 8
    )
    return mixed[None]


def solution(mesh):
    rows = P("section", "expert", None)
    slabs = P("section", "expert", None, None)
    return jax.shard_map(
        on_device,
        mesh=mesh,
        in_specs=(rows, P("section", None), rows, rows, rows, rows, slabs, slabs, slabs),
        out_specs=rows,
        check_vma=False,
    )
```

time: 156 us -> 64.6 us (0.41)
  waiting for transfers between devices: 113 us -> 20.8 us
  starting transfers between devices: 1.97 us -> 26.4 us
  matrix products: 18.2 us -> 0 us
  between operations: 13.3 us -> 0.14 us
  local copies, waits for them, and re-layouts: 0.18 us -> 9.52 us
  other arithmetic: 8.89 us -> 0 us
  Pallas kernels: 0 us -> 7.43 us
    reduce_scatter x2 -> x0, waiting for transfers between devices: 63.9 us -> none  [layer(): lax.psum_scatter(partial_value.astype(jnp.bfloat16), 'expert', scatter_di...]
    all_gather x2 -> x0, waiting for transfers between devices: 45.3 us -> none  [layer(): lax.all_gather(jnp.concatenate([normed, ids], axis=1), 'expert', axis=0,...]
    ppermute x1 -> x25, starting transfers between devices: 1.84 us -> 26.4 us  [the longest x6 10.1 us: experts(): arrived[k] = lax.ppermute(blocks[k], 'expert', to_expert(k))]
    dot_general x4 -> x0, matrix products: 18.2 us -> none  [the longest x2 11.7 us: layer(): partial_value = jnp.dot(hidden, w_down, preferred_element_type=jnp.float32)]
    ppermute x1 -> x25, waiting for transfers between devices: 4.07 us -> 20.8 us  [the longest x6 9.42 us: experts(): arrived[k] = lax.ppermute(blocks[k], 'expert', to_expert(k))]
    unnamed x14 -> x28, local copies, waits for them, and re-layouts: 0.04 us -> 9.52 us
    pallas_call x0 -> x7, Pallas kernels: none -> 7.43 us  [call(): pl.pallas_call(body, out_shape=outs, in_specs=[VMEM] * len(ins), out_spec...]
    convert_element_type x5 -> x0, other arithmetic: 2.79 us -> none  [the longest x2 1.11 us: normalize(): return (values * inv_scale * norm_scale[None, :]).astype(jnp.bfloat16)]
  transfers between devices with their start and end apart: 5 -> 25, of which waited for: 5 -> 13; matrix products, arithmetic and copies ran while one was open for 0% -> 0% of each run, Pallas kernels for 0% -> 0%
where the time goes in v2:
time: 64.6 us; the launch traced here: 64.3 us
  starting transfers between devices  26.4 us (41%)
  waiting for transfers between devices  20.8 us (32%)
  local copies, waits for them, and re-layouts  9.52 us (15%)
  Pallas kernels  7.43 us (12%)
    ppermute x6, starting transfers between devices, experts(): arrived[k] = lax.ppermute(blocks[k], 'expert', to_expert(k))  10.1 us
    unnamed x28, local copies, waits for them, and re-layouts  9.52 us
    ppermute x6, waiting for transfers between devices, experts(): arrived[k] = lax.ppermute(blocks[k], 'expert', to_expert(k))  9.42 us
    pallas_call x7, Pallas kernels, call(): pl.pallas_call(body, out_shape=outs, in_specs=[VMEM] * len(ins), out_spec...  7.43 us
    ppermute x4, starting transfers between devices, on_device(): lax.ppermute(sums[k], ('section', 'expert'), onward(k))  7.34 us
    ppermute x3, starting transfers between devices, on_device(): lax.ppermute(sums[k], 'expert', to_expert(k))  4.44 us
    ppermute x4, waiting for transfers between devices, on_device(): lax.ppermute(sums[k], ('section', 'expert'), onward(k))  4.11 us
    ppermute x3, waiting for transfers between devices, on_device(): lax.ppermute(sums[k], 'expert', to_expert(k))  3.25 us
  transfers between devices with their start and end apart: 25, of which 13 were waited for; matrix products, arithmetic and copies ran while one was open for 0% of the time, Pallas kernels for 0%

profile of v2, /device:TPU:0, one launch (start us, length us, event | category | flops | bytes accessed | tf_op | source)
XLA Modules:
  0.0 64.3 jit_solution(6356661070827762973)
XLA Ops:
  0.0 0.9 %copy-done.6 = bf16[1,16,4096]{2,1,0:T(8,128)(2,1)S(1)} copy-done((bf16[1,16,4096]{2,1,0:T(8,128)(2,1)S(1)}, bf16[1,16,4096]{2,1,0:T(8,128)(2,1)}, u32[]{:S(2)}) %copy-start.6) | copy-done | bytes 131096
  0.9 0.7 %copy-done.8 = f32[1,4096]{1,0:T(1,128)S(1)} copy-done((f32[1,4096]{1,0:T(1,128)S(1)}, f32[1,4096]{1,0:T(1,128)}, u32[]{:S(2)}) %copy-start.8) | copy-done | bytes 16408
  1.6 0.7 %copy-done.11 = s32[1,16,1]{1,2,0:T(1,128)S(1)} copy-done((s32[1,16,1]{1,2,0:T(1,128)S(1)}, s32[1,16,1]{1,2,0:T(1,128)}, u32[]{:S(2)}) %copy-start.11) | copy-done | bytes 88
  2.3 0.7 %copy-done.12 = f32[1,16,1]{1,2,0:T(1,128)S(1)} copy-done((f32[1,16,1]{1,2,0:T(1,128)S(1)}, f32[1,16,1]{1,2,0:T(1,128)}, u32[]{:S(2)}) %copy-start.12) | copy-done | bytes 88
  3.5 3.1 %collective-permute-start.2 = (bf16[16,1408]{1,0:T(8,128)(2,1)S(1)}, bf16[16,1408]{1,0:T(8,128)(2,1)S(1)}, u32[]{:S(2)}, u32[]{:S(2)}) collective-permute-start(bf16[16,1408]{1,0:T(8,128)(2,1)S(1)} %get-tuple-element.29), channel_id=1, source_target_pairs={{0,2},{1,3},{2,0},{3,1},{4,6},{5,7},{6,4},{7,5},{8,10},{9,11},{10,... | collective-permute-start | bytes 135176 | tf_op jit(solution)/shard_map/ppermute | solution.py:226
  6.6 2.6 %collective-permute-start.3 = (bf16[16,1408]{1,0:T(8,128)(2,1)S(1)}, bf16[16,1408]{1,0:T(8,128)(2,1)S(1)}, u32[]{:S(2)}, u32[]{:S(2)}) collective-permute-start(bf16[16,1408]{1,0:T(8,128)(2,1)S(1)} %get-tuple-element.30), channel_id=1, source_target_pairs={{0,4},{1,5},{2,6},{3,7},{4,0},{5,1},{6,2},{7,3},{8,12},{9,13},{10,... | collective-permute-start | bytes 135176 | tf_op jit(solution)/shard_map/ppermute | solution.py:226
  9.7 2.7 %collective-permute-done.3.refs_2_ = bf16[16,1408]{1,0:T(8,128)(2,1)S(1)} collective-permute-done((bf16[16,1408]{1,0:T(8,128)(2,1)S(1)}, bf16[16,1408]{1,0:T(8,128)(2,1)S(1)}, u32[]{:S(2)}, u32[]{:S(2)}) %collective-permute-start.3) | collective-permute-done | bytes 45088 | tf_op jit(solution)/shard_map/ppermute | solution.py:226
  12.4 2.6 %collective-permute-done.4.refs_3_ = bf16[16,1408]{1,0:T(8,128)(2,1)S(1)} collective-permute-done((bf16[16,1408]{1,0:T(8,128)(2,1)S(1)}, bf16[16,1408]{1,0:T(8,128)(2,1)S(1)}, u32[]{:S(2)}, u32[]{:S(2)}) %collective-permute-start.4) | collective-permute-done | bytes 45088 | tf_op jit(solution)/shard_map/ppermute | solution.py:226
  15.1 1.2 %collective-permute-done.8.refs_7_ = bf16[16,1408]{1,0:T(8,128)(2,1)S(1)} collective-permute-done((bf16[16,1408]{1,0:T(8,128)(2,1)S(1)}, bf16[16,1408]{1,0:T(8,128)(2,1)S(1)}, u32[]{:S(2)}, u32[]{:S(2)}) %collective-permute-start.8) | collective-permute-done | bytes 45088 | tf_op jit(solution)/shard_map/ppermute | solution.py:230
  16.3 2.2 %copy-done = bf16[1,1,4096,512]{3,2,1,0:T(8,128)(2,1)S(1)} copy-done((bf16[1,1,4096,512]{3,2,1,0:T(8,128)(2,1)S(1)}, bf16[1,1,4096,512]{3,2,1,0:T(8,128)(2,1)}, u32[]{:S(2)}) %copy-start) | copy-done | bytes 4194328
  18.5 2.2 %copy-done.2 = bf16[1,1,4096,512]{3,2,1,0:T(8,128)(2,1)S(1)} copy-done((bf16[1,1,4096,512]{3,2,1,0:T(8,128)(2,1)S(1)}, bf16[1,1,4096,512]{3,2,1,0:T(8,128)(2,1)}, u32[]{:S(2)}) %copy-start.2) | copy-done | bytes 4194328
  20.7 2.2 %copy-done.4 = bf16[1,1,512,4096]{3,2,1,0:T(8,128)(2,1)S(1)} copy-done((bf16[1,1,512,4096]{3,2,1,0:T(8,128)(2,1)S(1)}, bf16[1,1,512,4096]{3,2,1,0:T(8,128)(2,1)}, u32[]{:S(2)}) %copy-start.4) | copy-done | bytes 4194328
  22.9 2.5 %shard_map.92 = (bf16[64,1408]{1,0:T(8,128)(2,1)S(1)}, bf16[64,1408]{1,0:T(8,128)(2,1)S(1)}) custom-call(bf16[4096,512]{1,0:T(8,128)(2,1)S(1)} %bitcast.9, bf16[4096,512]{1,0:T(8,128)(2,1)S(1)} %bitcast.11, bf16[512,4096]{1,0:T(8,128)(2,1)S(1)} %bitcast.13, bf16[16,1408]{1,0:T(8,128)(2,1)S(1)} %get-tuple-element.28.refs_0_, ...), custom_call_target="tpu_custom_call" | custom-call | flops 603979776 | bytes 13303808 | tf_op jit(solution)/shard_map/pallas_call | solution.py:185
  25.6 1.5 %collective-permute-start = (bf16[16,4096]{1,0:T(8,128)(2,1)S(1)}, bf16[16,4096]{1,0:T(8,128)(2,1)S(1)}, u32[]{:S(2)}, u32[]{:S(2)}) collective-permute-start(bf16[16,4096]{1,0:T(8,128)(2,1)S(1)} %bitcast.16), channel_id=1, source_target_pairs={{0,8},{8,16},{16,24},{24,0},{1,9},{9,17},{17,25},{25,1},{2,10},{10... | collective-permute-start | bytes 393224 | tf_op jit(solution)/shard_map/ppermute | solution.py:252
  27.1 1.5 %collective-permute-start.1 = (f32[16,128]{1,0:T(8,128)S(1)}, f32[16,128]{1,0:T(8,128)S(1)}, u32[]{:S(2)}, u32[]{:S(2)}) collective-permute-start(f32[16,128]{1,0:T(8,128)S(1)} %get-tuple-element.27), channel_id=1, source_target_pairs={{0,8},{8,16},{16,24},{24,0},{1,9},{9,17},{17,25},{25,1},{2,10},{10... | collective-permute-start | bytes 24584 | tf_op jit(solution)/shard_map/ppermute | solution.py:251
  28.6 1.6 %collective-permute-start.10 = (bf16[16,1408]{1,0:T(8,128)(2,1)S(1)}, bf16[16,1408]{1,0:T(8,128)(2,1)S(1)}, u32[]{:S(2)}, u32[]{:S(2)}) collective-permute-start(bf16[16,1408]{1,0:T(8,128)(2,1)S(1)} %get-tuple-element.34), channel_id=1, source_target_pairs={{0,8},{1,9},{2,10},{3,11},{4,12},{5,13},{6,14},{7,15},{8,16},{9,17... | collective-permute-start | bytes 135176 | tf_op jit(solution)/shard_map/ppermute | solution.py:254
  30.2 2.3 %collective-permute-start.12 = (bf16[16,1408]{1,0:T(8,128)(2,1)S(1)}, bf16[16,1408]{1,0:T(8,128)(2,1)S(1)}, u32[]{:S(2)}, u32[]{:S(2)}) collective-permute-start(bf16[16,1408]{1,0:T(8,128)(2,1)S(1)} %get-tuple-element.36), channel_id=1, source_target_pairs={{0,12},{1,13},{2,14},{3,15},{4,8},{5,9},{6,10},{7,11},{8,20},{9,21... | collective-permute-start | bytes 135176 | tf_op jit(solution)/shard_map/ppermute | solution.py:254
  32.8 3.5 %collective-permute-start.13 = (bf16[16,1408]{1,0:T(8,128)(2,1)S(1)}, bf16[16,1408]{1,0:T(8,128)(2,1)S(1)}, u32[]{:S(2)}, u32[]{:S(2)}) collective-permute-start(bf16[16,1408]{1,0:T(8,128)(2,1)S(1)} %get-tuple-element.37), channel_id=1, source_target_pairs={{0,14},{1,15},{2,12},{3,13},{4,10},{5,11},{6,8},{7,9},{8,22},{9,23... | collective-permute-start | bytes 135176 | tf_op jit(solution)/shard_map/ppermute | solution.py:254
  36.4 1.0 %collective-permute-done.12.b2 = bf16[16,1408]{1,0:T(8,128)(2,1)S(1)} collective-permute-done((bf16[16,1408]{1,0:T(8,128)(2,1)S(1)}, bf16[16,1408]{1,0:T(8,128)(2,1)S(1)}, u32[]{:S(2)}, u32[]{:S(2)}) %collective-permute-start.12) | collective-permute-done | bytes 45088 | tf_op jit(solution)/shard_map/ppermute | solution.py:254
  37.4 3.1 %collective-permute-done.13.b3 = bf16[16,1408]{1,0:T(8,128)(2,1)S(1)} collective-permute-done((bf16[16,1408]{1,0:T(8,128)(2,1)S(1)}, bf16[16,1408]{1,0:T(8,128)(2,1)S(1)}, u32[]{:S(2)}, u32[]{:S(2)}) %collective-permute-start.13) | collective-permute-done | bytes 45088 | tf_op jit(solution)/shard_map/ppermute | solution.py:254
  41.2 3.1 %collective-permute-start.15 = (bf16[16,1408]{1,0:T(8,128)(2,1)S(1)}, bf16[16,1408]{1,0:T(8,128)(2,1)S(1)}, u32[]{:S(2)}, u32[]{:S(2)}) collective-permute-start(bf16[16,1408]{1,0:T(8,128)(2,1)S(1)} %get-tuple-element.41), channel_id=1, source_target_pairs={{0,4},{1,5},{2,6},{3,7},{4,0},{5,1},{6,2},{7,3},{8,12},{9,13},{10,... | collective-permute-start | bytes 135176 | tf_op jit(solution)/shard_map/ppermute | solution.py:226
  44.4 1.2 %collective-permute-start.16 = (bf16[16,1408]{1,0:T(8,128)(2,1)S(1)}, bf16[16,1408]{1,0:T(8,128)(2,1)S(1)}, u32[]{:S(2)}, u32[]{:S(2)}) collective-permute-start(bf16[16,1408]{1,0:T(8,128)(2,1)S(1)} %get-tuple-element.42), channel_id=1, source_target_pairs={{0,6},{1,7},{2,4},{3,5},{4,2},{5,3},{6,0},{7,1},{8,14},{9,15},{10,... | collective-permute-start | bytes 135176 | tf_op jit(solution)/shard_map/ppermute | solution.py:226
  46.1 0.8 %collective-permute-done.15.refs_2_ = bf16[16,1408]{1,0:T(8,128)(2,1)S(1)} collective-permute-done((bf16[16,1408]{1,0:T(8,128)(2,1)S(1)}, bf16[16,1408]{1,0:T(8,128)(2,1)S(1)}, u32[]{:S(2)}, u32[]{:S(2)}) %collective-permute-start.15) | collective-permute-done | bytes 45088 | tf_op jit(solution)/shard_map/ppermute | solution.py:226
  46.9 3.3 %collective-permute-done.16.refs_3_ = bf16[16,1408]{1,0:T(8,128)(2,1)S(1)} collective-permute-done((bf16[16,1408]{1,0:T(8,128)(2,1)S(1)}, bf16[16,1408]{1,0:T(8,128)(2,1)S(1)}, u32[]{:S(2)}, u32[]{:S(2)}) %collective-permute-start.16) | collective-permute-done | bytes 45088 | tf_op jit(solution)/shard_map/ppermute | solution.py:226
  50.2 1.2 %collective-permute-done.20.refs_7_ = bf16[16,1408]{1,0:T(8,128)(2,1)S(1)} collective-permute-done((bf16[16,1408]{1,0:T(8,128)(2,1)S(1)}, bf16[16,1408]{1,0:T(8,128)(2,1)S(1)}, u32[]{:S(2)}, u32[]{:S(2)}) %collective-permute-start.20) | collective-permute-done | bytes 45088 | tf_op jit(solution)/shard_map/ppermute | solution.py:230
  51.4 2.5 %shard_map.95 = (bf16[64,1408]{1,0:T(8,128)(2,1)S(1)}, bf16[64,1408]{1,0:T(8,128)(2,1)S(1)}) custom-call(bf16[4096,512]{1,0:T(8,128)(2,1)S(1)} %bitcast.10, bf16[4096,512]{1,0:T(8,128)(2,1)S(1)} %bitcast.12, bf16[512,4096]{1,0:T(8,128)(2,1)S(1)} %bitcast.14, bf16[16,1408]{1,0:T(8,128)(2,1)S(1)} %get-tuple-element.39.refs_0_, ...), custom_call_target="tpu_custom_call" | custom-call | flops 603979776 | bytes 13303808 | tf_op jit(solution)/shard_map/pallas_call | solution.py:185
  54.1 1.3 %collective-permute-done.21.refs_1_ = bf16[64,1408]{1,0:T(8,128)(2,1)S(1)} collective-permute-done((bf16[64,1408]{1,0:T(8,128)(2,1)S(1)}, bf16[64,1408]{1,0:T(8,128)(2,1)S(1)}, u32[]{:S(2)}, u32[]{:S(2)}) %collective-permute-start.21) | collective-permute-done | bytes 180256 | tf_op jit(solution)/shard_map/ppermute | solution.py:241
  55.5 1.8 %collective-permute-start.23 = (bf16[16,1408]{1,0:T(8,128)(2,1)S(1)}, bf16[16,1408]{1,0:T(8,128)(2,1)S(1)}, u32[]{:S(2)}, u32[]{:S(2)}) collective-permute-start(bf16[16,1408]{1,0:T(8,128)(2,1)S(1)} %get-tuple-element.47), channel_id=1, source_target_pairs={{0,4},{1,5},{2,6},{3,7},{4,0},{5,1},{6,2},{7,3},{8,12},{9,13},{10,... | collective-permute-start | bytes 135176 | tf_op jit(solution)/shard_map/ppermute | solution.py:262
  57.3 2.6 %collective-permute-start.24 = (bf16[16,1408]{1,0:T(8,128)(2,1)S(1)}, bf16[16,1408]{1,0:T(8,128)(2,1)S(1)}, u32[]{:S(2)}, u32[]{:S(2)}) collective-permute-start(bf16[16,1408]{1,0:T(8,128)(2,1)S(1)} %get-tuple-element.48), channel_id=1, source_target_pairs={{0,6},{1,7},{2,4},{3,5},{4,2},{5,3},{6,0},{7,1},{8,14},{9,15},{10,... | collective-permute-start | bytes 135176 | tf_op jit(solution)/shard_map/ppermute | solution.py:262
  60.0 1.1 %collective-permute-done.23.b2 = bf16[16,1408]{1,0:T(8,128)(2,1)S(1)} collective-permute-done((bf16[16,1408]{1,0:T(8,128)(2,1)S(1)}, bf16[16,1408]{1,0:T(8,128)(2,1)S(1)}, u32[]{:S(2)}, u32[]{:S(2)}) %collective-permute-start.23) | collective-permute-done | bytes 45088 | tf_op jit(solution)/shard_map/ppermute | solution.py:262
  61.2 2.0 %collective-permute-done.24.b3 = bf16[16,1408]{1,0:T(8,128)(2,1)S(1)} collective-permute-done((bf16[16,1408]{1,0:T(8,128)(2,1)S(1)}, bf16[16,1408]{1,0:T(8,128)(2,1)S(1)}, u32[]{:S(2)}, u32[]{:S(2)}) %collective-permute-start.24) | collective-permute-done | bytes 45088 | tf_op jit(solution)/shard_map/ppermute | solution.py:262
  63.2 1.1 %shard_map.97 = bf16[16,4096]{1,0:T(8,128)(2,1)} custom-call(bf16[16,4096]{1,0:T(8,128)(2,1)S(1)} %get-tuple-element.38.x_ref, bf16[16,1408]{1,0:T(8,128)(2,1)S(1)} %get-tuple-element.45.b0, bf16[16,1408]{1,0:T(8,128)(2,1)S(1)} %collective-permute-done.22.b1, bf16[16,1408]{1,0:T(8,128)(2,1)S(1)} %collective-permute-done.23.b2, ...), custom_call_target="tpu_custom_call" | custom-call | bytes 442496 | tf_op jit(solution)/shard_map/pallas_call | solution.py:185
  (53 shorter events, 3.5 us)
Async XLA Ops:
  3.5 5.7 %collective-permute-start.2 = (bf16[16,1408]{1,0:T(8,128)(2,1)S(1)}, bf16[16,1408]{1,0:T(8,128)(2,1)S(1)}, u32[]{:S(2)}, u32[]{:S(2)}) collective-permute-start(bf16[16,1408]{1,0:T(8,128)(2,1)S(1)} %get-tuple-element.29), channel_id=1, source_target_pairs={{0,2},{1,3},{2,0},{3,1},{4,6},{5,7},{6,4},{7,5},{8,10},{9,11},{10,... | collective-permute-start | bytes 135176 | tf_op jit(solution)/shard_map/ppermute | solution.py:226
  6.6 5.8 %collective-permute-start.3 = (bf16[16,1408]{1,0:T(8,128)(2,1)S(1)}, bf16[16,1408]{1,0:T(8,128)(2,1)S(1)}, u32[]{:S(2)}, u32[]{:S(2)}) collective-permute-start(bf16[16,1408]{1,0:T(8,128)(2,1)S(1)} %get-tuple-element.30), channel_id=1, source_target_pairs={{0,4},{1,5},{2,6},{3,7},{4,0},{5,1},{6,2},{7,3},{8,12},{9,13},{10,... | collective-permute-start | bytes 135176 | tf_op jit(solution)/shard_map/ppermute | solution.py:226
  9.2 5.8 %collective-permute-start.4 = (bf16[16,1408]{1,0:T(8,128)(2,1)S(1)}, bf16[16,1408]{1,0:T(8,128)(2,1)S(1)}, u32[]{:S(2)}, u32[]{:S(2)}) collective-permute-start(bf16[16,1408]{1,0:T(8,128)(2,1)S(1)} %get-tuple-element.31), channel_id=1, source_target_pairs={{0,6},{1,7},{2,4},{3,5},{4,2},{5,3},{6,0},{7,1},{8,14},{9,15},{10,... | collective-permute-start | bytes 135176 | tf_op jit(solution)/shard_map/ppermute | solution.py:226
  9.2 5.8 %collective-permute-start.5 = (bf16[16,1408]{1,0:T(8,128)(2,1)S(1)}, bf16[16,1408]{1,0:T(8,128)(2,1)S(1)}, u32[]{:S(2)}, u32[]{:S(2)}) collective-permute-start(bf16[16,1408]{1,0:T(8,128)(2,1)S(1)} %get-tuple-element.28.refs_0_), channel_id=1, source_target_pairs={{0,1},{1,0},{2,3},{3,2},{4,5},{5,4},{6,7},{7,6},{8,9},{9,8},{10,11... | collective-permute-start | bytes 135176 | tf_op jit(solution)/shard_map/ppermute | solution.py:230
  9.2 5.8 %collective-permute-start.6 = (bf16[16,1408]{1,0:T(8,128)(2,1)S(1)}, bf16[16,1408]{1,0:T(8,128)(2,1)S(1)}, u32[]{:S(2)}, u32[]{:S(2)}) collective-permute-start(bf16[16,1408]{1,0:T(8,128)(2,1)S(1)} %collective-permute-done.2.refs_1_), channel_id=1, source_target_pairs={{0,1},{1,0},{2,3},{3,2},{4,5},{5,4},{6,7},{7,6},{8,9},{9,8},{10,11... | collective-permute-start | bytes 135176 | tf_op jit(solution)/shard_map/ppermute | solution.py:230
  12.4 2.7 %collective-permute-start.7 = (bf16[16,1408]{1,0:T(8,128)(2,1)S(1)}, bf16[16,1408]{1,0:T(8,128)(2,1)S(1)}, u32[]{:S(2)}, u32[]{:S(2)}) collective-permute-start(bf16[16,1408]{1,0:T(8,128)(2,1)S(1)} %collective-permute-done.3.refs_2_), channel_id=1, source_target_pairs={{0,1},{1,0},{2,3},{3,2},{4,5},{5,4},{6,7},{7,6},{8,9},{9,8},{10,11... | collective-permute-start | bytes 135176 | tf_op jit(solution)/shard_map/ppermute | solution.py:230
  15.1 1.2 %collective-permute-start.8 = (bf16[16,1408]{1,0:T(8,128)(2,1)S(1)}, bf16[16,1408]{1,0:T(8,128)(2,1)S(1)}, u32[]{:S(2)}, u32[]{:S(2)}) collective-permute-start(bf16[16,1408]{1,0:T(8,128)(2,1)S(1)} %collective-permute-done.4.refs_3_), channel_id=1, source_target_pairs={{0,1},{1,0},{2,3},{3,2},{4,5},{5,4},{6,7},{7,6},{8,9},{9,8},{10,11... | collective-permute-start | bytes 135176 | tf_op jit(solution)/shard_map/ppermute | solution.py:230
  22.8 2.8 %copy-start.7 = (bf16[1,16,4096]{2,1,0:T(8,128)(2,1)S(1)}, bf16[1,16,4096]{2,1,0:T(8,128)(2,1)}, u32[]{:S(2)}) copy-start(bf16[1,16,4096]{2,1,0:T(8,128)(2,1)} %param.9) | copy-start | bytes 393220
  22.8 17.6 %copy-start.9 = (f32[1,4096]{1,0:T(1,128)S(1)}, f32[1,4096]{1,0:T(1,128)}, u32[]{:S(2)}) copy-start(f32[1,4096]{1,0:T(1,128)} %gain_ref.3) | copy-start | bytes 49156
  22.9 17.6 %copy-start.10 = (s32[1,16,1]{1,2,0:T(1,128)S(1)}, s32[1,16,1]{1,2,0:T(1,128)}, u32[]{:S(2)}) copy-start(s32[1,16,1]{1,2,0:T(1,128)} %param.13) | copy-start | bytes 196
  22.9 28.6 %copy-start.1 = (bf16[1,1,4096,512]{3,2,1,0:T(8,128)(2,1)S(1)}, bf16[1,1,4096,512]{3,2,1,0:T(8,128)(2,1)}, u32[]{:S(2)}) copy-start(bf16[1,1,4096,512]{3,2,1,0:T(8,128)(2,1)} %param.15) | copy-start | bytes 12582916
  22.9 28.6 %copy-start.3 = (bf16[1,1,4096,512]{3,2,1,0:T(8,128)(2,1)S(1)}, bf16[1,1,4096,512]{3,2,1,0:T(8,128)(2,1)}, u32[]{:S(2)}) copy-start(bf16[1,1,4096,512]{3,2,1,0:T(8,128)(2,1)} %param.16) | copy-start | bytes 12582916
  22.9 28.6 %copy-start.5 = (bf16[1,1,512,4096]{3,2,1,0:T(8,128)(2,1)S(1)}, bf16[1,1,512,4096]{3,2,1,0:T(8,128)(2,1)}, u32[]{:S(2)}) copy-start(bf16[1,1,512,4096]{3,2,1,0:T(8,128)(2,1)} %param.17) | copy-start | bytes 12582916
  25.4 3.2 %collective-permute-start.9 = (bf16[64,1408]{1,0:T(8,128)(2,1)S(1)}, bf16[64,1408]{1,0:T(8,128)(2,1)S(1)}, u32[]{:S(2)}, u32[]{:S(2)}) collective-permute-start(bf16[64,1408]{1,0:T(8,128)(2,1)S(1)} %get-tuple-element.33), channel_id=1, source_target_pairs={{0,1},{1,0},{2,3},{3,2},{4,5},{5,4},{6,7},{7,6},{8,9},{9,8},{10,11... | collective-permute-start | bytes 540680 | tf_op jit(solution)/shard_map/ppermute | solution.py:241
  25.6 10.7 %collective-permute-start = (bf16[16,4096]{1,0:T(8,128)(2,1)S(1)}, bf16[16,4096]{1,0:T(8,128)(2,1)S(1)}, u32[]{:S(2)}, u32[]{:S(2)}) collective-permute-start(bf16[16,4096]{1,0:T(8,128)(2,1)S(1)} %bitcast.16), channel_id=1, source_target_pairs={{0,8},{8,16},{16,24},{24,0},{1,9},{9,17},{17,25},{25,1},{2,10},{10... | collective-permute-start | bytes 393224 | tf_op jit(solution)/shard_map/ppermute | solution.py:252
  27.1 5.7 %collective-permute-start.1 = (f32[16,128]{1,0:T(8,128)S(1)}, f32[16,128]{1,0:T(8,128)S(1)}, u32[]{:S(2)}, u32[]{:S(2)}) collective-permute-start(f32[16,128]{1,0:T(8,128)S(1)} %get-tuple-element.27), channel_id=1, source_target_pairs={{0,8},{8,16},{16,24},{24,0},{1,9},{9,17},{17,25},{25,1},{2,10},{10... | collective-permute-start | bytes 24584 | tf_op jit(solution)/shard_map/ppermute | solution.py:251
  28.6 7.7 %collective-permute-start.10 = (bf16[16,1408]{1,0:T(8,128)(2,1)S(1)}, bf16[16,1408]{1,0:T(8,128)(2,1)S(1)}, u32[]{:S(2)}, u32[]{:S(2)}) collective-permute-start(bf16[16,1408]{1,0:T(8,128)(2,1)S(1)} %get-tuple-element.34), channel_id=1, source_target_pairs={{0,8},{1,9},{2,10},{3,11},{4,12},{5,13},{6,14},{7,15},{8,16},{9,17... | collective-permute-start | bytes 135176 | tf_op jit(solution)/shard_map/ppermute | solution.py:254
  30.2 6.2 %collective-permute-start.11 = (bf16[16,1408]{1,0:T(8,128)(2,1)S(1)}, bf16[16,1408]{1,0:T(8,128)(2,1)S(1)}, u32[]{:S(2)}, u32[]{:S(2)}) collective-permute-start(bf16[16,1408]{1,0:T(8,128)(2,1)S(1)} %get-tuple-element.35), channel_id=1, source_target_pairs={{0,10},{1,11},{2,8},{3,9},{4,14},{5,15},{6,12},{7,13},{8,18},{9,19... | collective-permute-start | bytes 135176 | tf_op jit(solution)/shard_map/ppermute | solution.py:254
  30.2 7.2 %collective-permute-start.12 = (bf16[16,1408]{1,0:T(8,128)(2,1)S(1)}, bf16[16,1408]{1,0:T(8,128)(2,1)S(1)}, u32[]{:S(2)}, u32[]{:S(2)}) collective-permute-start(bf16[16,1408]{1,0:T(8,128)(2,1)S(1)} %get-tuple-element.36), channel_id=1, source_target_pairs={{0,12},{1,13},{2,14},{3,15},{4,8},{5,9},{6,10},{7,11},{8,20},{9,21... | collective-permute-start | bytes 135176 | tf_op jit(solution)/shard_map/ppermute | solution.py:254
  32.8 7.6 %collective-permute-start.13 = (bf16[16,1408]{1,0:T(8,128)(2,1)S(1)}, bf16[16,1408]{1,0:T(8,128)(2,1)S(1)}, u32[]{:S(2)}, u32[]{:S(2)}) collective-permute-start(bf16[16,1408]{1,0:T(8,128)(2,1)S(1)} %get-tuple-element.37), channel_id=1, source_target_pairs={{0,14},{1,15},{2,12},{3,13},{4,10},{5,11},{6,8},{7,9},{8,22},{9,23... | collective-permute-start | bytes 135176 | tf_op jit(solution)/shard_map/ppermute | solution.py:254
  41.1 4.5 %collective-permute-start.14 = (bf16[16,1408]{1,0:T(8,128)(2,1)S(1)}, bf16[16,1408]{1,0:T(8,128)(2,1)S(1)}, u32[]{:S(2)}, u32[]{:S(2)}) collective-permute-start(bf16[16,1408]{1,0:T(8,128)(2,1)S(1)} %get-tuple-element.40), channel_id=1, source_target_pairs={{0,2},{1,3},{2,0},{3,1},{4,6},{5,7},{6,4},{7,5},{8,10},{9,11},{10,... | collective-permute-start | bytes 135176 | tf_op jit(solution)/shard_map/ppermute | solution.py:226
  41.2 5.7 %collective-permute-start.15 = (bf16[16,1408]{1,0:T(8,128)(2,1)S(1)}, bf16[16,1408]{1,0:T(8,128)(2,1)S(1)}, u32[]{:S(2)}, u32[]{:S(2)}) collective-permute-start(bf16[16,1408]{1,0:T(8,128)(2,1)S(1)} %get-tuple-element.41), channel_id=1, source_target_pairs={{0,4},{1,5},{2,6},{3,7},{4,0},{5,1},{6,2},{7,3},{8,12},{9,13},{10,... | collective-permute-start | bytes 135176 | tf_op jit(solution)/shard_map/ppermute | solution.py:226
  44.4 5.8 %collective-permute-start.16 = (bf16[16,1408]{1,0:T(8,128)(2,1)S(1)}, bf16[16,1408]{1,0:T(8,128)(2,1)S(1)}, u32[]{:S(2)}, u32[]{:S(2)}) collective-permute-start(bf16[16,1408]{1,0:T(8,128)(2,1)S(1)} %get-tuple-element.42), channel_id=1, source_target_pairs={{0,6},{1,7},{2,4},{3,5},{4,2},{5,3},{6,0},{7,1},{8,14},{9,15},{10,... | collective-permute-start | bytes 135176 | tf_op jit(solution)/shard_map/ppermute | solution.py:226
  45.6 17.6 %copy-start.13 = (f32[1,16,1]{1,2,0:T(1,128)S(1)}, f32[1,16,1]{1,2,0:T(1,128)}, u32[]{:S(2)}) copy-start(f32[1,16,1]{1,2,0:T(1,128)} %param.14) | copy-start | bytes 196
  45.6 4.6 %collective-permute-start.17 = (bf16[16,1408]{1,0:T(8,128)(2,1)S(1)}, bf16[16,1408]{1,0:T(8,128)(2,1)S(1)}, u32[]{:S(2)}, u32[]{:S(2)}) collective-permute-start(bf16[16,1408]{1,0:T(8,128)(2,1)S(1)} %get-tuple-element.39.refs_0_), channel_id=1, source_target_pairs={{0,1},{1,0},{2,3},{3,2},{4,5},{5,4},{6,7},{7,6},{8,9},{9,8},{10,11... | collective-permute-start | bytes 135176 | tf_op jit(solution)/shard_map/ppermute | solution.py:230
  45.6 4.6 %collective-permute-start.18 = (bf16[16,1408]{1,0:T(8,128)(2,1)S(1)}, bf16[16,1408]{1,0:T(8,128)(2,1)S(1)}, u32[]{:S(2)}, u32[]{:S(2)}) collective-permute-start(bf16[16,1408]{1,0:T(8,128)(2,1)S(1)} %collective-permute-done.14.refs_1_), channel_id=1, source_target_pairs={{0,1},{1,0},{2,3},{3,2},{4,5},{5,4},{6,7},{7,6},{8,9},{9,8},{10,11... | collective-permute-start | bytes 135176 | tf_op jit(solution)/shard_map/ppermute | solution.py:230
  46.9 3.4 %collective-permute-start.19 = (bf16[16,1408]{1,0:T(8,128)(2,1)S(1)}, bf16[16,1408]{1,0:T(8,128)(2,1)S(1)}, u32[]{:S(2)}, u32[]{:S(2)}) collective-permute-start(bf16[16,1408]{1,0:T(8,128)(2,1)S(1)} %collective-permute-done.15.refs_2_), channel_id=1, source_target_pairs={{0,1},{1,0},{2,3},{3,2},{4,5},{5,4},{6,7},{7,6},{8,9},{9,8},{10,11... | collective-permute-start | bytes 135176 | tf_op jit(solution)/shard_map/ppermute | solution.py:230
  50.2 1.2 %collective-permute-start.20 = (bf16[16,1408]{1,0:T(8,128)(2,1)S(1)}, bf16[16,1408]{1,0:T(8,128)(2,1)S(1)}, u32[]{:S(2)}, u32[]{:S(2)}) collective-permute-start(bf16[16,1408]{1,0:T(8,128)(2,1)S(1)} %collective-permute-done.16.refs_3_), channel_id=1, source_target_pairs={{0,1},{1,0},{2,3},{3,2},{4,5},{5,4},{6,7},{7,6},{8,9},{9,8},{10,11... | collective-permute-start | bytes 135176 | tf_op jit(solution)/shard_map/ppermute | solution.py:230
  53.9 1.5 %collective-permute-start.21 = (bf16[64,1408]{1,0:T(8,128)(2,1)S(1)}, bf16[64,1408]{1,0:T(8,128)(2,1)S(1)}, u32[]{:S(2)}, u32[]{:S(2)}) collective-permute-start(bf16[64,1408]{1,0:T(8,128)(2,1)S(1)} %get-tuple-element.44), channel_id=1, source_target_pairs={{0,1},{1,0},{2,3},{3,2},{4,5},{5,4},{6,7},{7,6},{8,9},{9,8},{10,11... | collective-permute-start | bytes 540680 | tf_op jit(solution)/shard_map/ppermute | solution.py:241
  55.4 4.6 %collective-permute-start.22 = (bf16[16,1408]{1,0:T(8,128)(2,1)S(1)}, bf16[16,1408]{1,0:T(8,128)(2,1)S(1)}, u32[]{:S(2)}, u32[]{:S(2)}) collective-permute-start(bf16[16,1408]{1,0:T(8,128)(2,1)S(1)} %get-tuple-element.46), channel_id=1, source_target_pairs={{0,2},{1,3},{2,0},{3,1},{4,6},{5,7},{6,4},{7,5},{8,10},{9,11},{10,... | collective-permute-start | bytes 135176 | tf_op jit(solution)/shard_map/ppermute | solution.py:262
  55.5 5.6 %collective-permute-start.23 = (bf16[16,1408]{1,0:T(8,128)(2,1)S(1)}, bf16[16,1408]{1,0:T(8,128)(2,1)S(1)}, u32[]{:S(2)}, u32[]{:S(2)}) collective-permute-start(bf16[16,1408]{1,0:T(8,128)(2,1)S(1)} %get-tuple-element.47), channel_id=1, source_target_pairs={{0,4},{1,5},{2,6},{3,7},{4,0},{5,1},{6,2},{7,3},{8,12},{9,13},{10,... | collective-permute-start | bytes 135176 | tf_op jit(solution)/shard_map/ppermute | solution.py:262
  57.3 5.8 %collective-permute-start.24 = (bf16[16,1408]{1,0:T(8,128)(2,1)S(1)}, bf16[16,1408]{1,0:T(8,128)(2,1)S(1)}, u32[]{:S(2)}, u32[]{:S(2)}) collective-permute-start(bf16[16,1408]{1,0:T(8,128)(2,1)S(1)} %get-tuple-element.48), channel_id=1, source_target_pairs={{0,6},{1,7},{2,4},{3,5},{4,2},{5,3},{6,0},{7,1},{8,14},{9,15},{10,... | collective-permute-start | bytes 135176 | tf_op jit(solution)/shard_map/ppermute | solution.py:262
  (7 other events, 9.5 us)
